TPU v7x, 128 devices: a whole 4x4x4 slice. The times are simulated.
128 devices in a mesh: dp: 8 (over y, z_lo), rec: 16 (over x, z_hi, core).
Axes of the slice: x: 4, y: 4, z: 4 (z_hi: 2, z_lo: 2; z = z_hi * 2 + z_lo), core: 2. Of those that a mesh axis runs over, the one named last changes fastest.
Arguments:
- grad_parts: float32 [8, 16, 512, 7168], P('dp', 'rec'), may hold values from -6 to 6
- params: float32 [16, 512, 7168], P('rec', 'dp'), may hold values from -6 to 6
- first_moment: float32 [16, 512, 7168], P('rec', 'dp'), may hold values from -4 to 4
- second_moment: float32 [16, 512, 7168], P('rec', 'dp'), may hold values from 0.01 to 1
- generator: float32 [4, 16], replicated, may hold values from -1 to 1
Outputs:
- new_params: float32 [16, 512, 7168], P('rec', 'dp')
- new_first: float32 [16, 512, 7168], P('rec', 'dp')
- new_second: float32 [16, 512, 7168], P('rec', 'dp')
- parity: float32 [8, 16, 3, 16, 7168], P('dp', 'rec')
All inputs are finite; a program needn't handle non-finite values.
Results may differ from a plain program's by a relative error of at most 0.000098.
Values sent between devices are 32-bit elements; how exact they have to be, the bound alone decides.
A program may use at most 192 MiB of HBM per device.

v0:
```python
import jax
import jax.numpy as jnp
from jax import lax
from jax.sharding import PartitionSpec as P


def per_device(grad_parts, params, first_moment, second_moment, generator):
    grad = lax.psum_scatter(grad_parts, "dp", scatter_dimension=2, tiled=True)
    grad = grad.reshape(params.shape)
    new_first = 0.9 * first_moment + 0.1 * grad
    new_second = 0.999 * second_moment + 0.001 * grad * grad
    bias_one = 1.0 - 0.9**10
    bias_two = 1.0 - 0.999**10
    step_dir = new_first / bias_one / (jnp.sqrt(new_second / bias_two) + 1e-08) + 0.1 * params
    new_params = params - 0.001 * step_dir
    members = lax.axis_size("rec")
    blocks = generator.shape[0]
    owners = members // blocks
    width = params.shape[2]
    piece_rows = params.shape[1] // owners
    member = lax.axis_index("rec")

    def split_rows(field):
        return field.reshape(owners, piece_rows, width)

    stacked = jnp.stack(
        [
            split_rows(step_dir),
            split_rows(grad - first_moment),
            split_rows(grad * grad - second_moment),
        ],
        axis=1,
    )
    column = lax.dynamic_slice_in_dim(generator, member, 1, 1).reshape(blocks, 1, 1, 1, 1)
    weighted = (column * stacked[None]).reshape(members, 3, piece_rows, width)
    owned = lax.psum_scatter(weighted, "rec", scatter_dimension=0, tiled=True)
    parity = owned.reshape(1, 1, 3, piece_rows, width)
    return (new_params, new_first, new_second, parity)


def solution(mesh):
    in_specs = (
        P("dp", "rec", None, None),
        P("rec", "dp", None),
        P("rec", "dp", None),
        P("rec", "dp", None),
        P(),
    )
    out_specs = (
        P("rec", "dp", None),
        P("rec", "dp", None),
        P("rec", "dp", None),
        P("dp", "rec", None, None, None),
    )
    return jax.shard_map(
        per_device, mesh=mesh, in_specs=in_specs, out_specs=out_specs, check_vma=False
    )
```

profile of v0, /device:TPU:1, one launch (start us, length us, event | category | flops | bytes accessed | tf_op | source)
XLA Modules:
  0.0 497.1 jit_solution(7157441999538916870)
XLA Ops:
  7.2 0.0 copy-start
  7.2 0.0 copy-start.1
  7.2 0.0 reduce-scatter.3.cloned.1.call-start
  7.2 0.7 reduce-scatter.3.cloned.1.call-update
  7.9 0.0 reduce-scatter.5.cloned.1.call-start
  8.0 0.0 copy-done
  8.0 0.2 dynamic-slice_reduce_fusion
  8.2 0.1 mul.94
  8.2 0.1 mul.95
  8.3 293.0 %reduce-scatter.3.cloned.1.call-done = f32[1,1,64,7168]{3,2,1,0:T(8,128)} async-done(((f32[1,1,512,7168]{3,2,1,0:T(8,128)}), f32[1,1,64,7168]{3,2,1,0:T(8,128)}) %reduce-scatter.3.cloned.1.call-update) | async-done | bytes 1835024 | tf_op jit(solution)/shard_map/reduce_scatter | solution.py:8
  301.4 0.0 copy-done.1
  301.4 6.2 %multiply_subtract_fusion = (f32[1,64,7168]{2,1,0:T(8,128)}, f32[1,64,7168]{2,1,0:T(8,128)S(1)}, f32[1,64,7168]{2,1,0:T(8,128)}, f32[1,64,7168]{2,1,0:T(8,128)},...) fusion(f32[1,64,7168]{2,1,0:T(8,128)S(1)} %copy-done.1, f32[1,1,64,7168]{3,2,1,0:T(8,128)} %reduce-scatter.3.cloned.1.call-done, ...), kind=kLoop, calls=%fused_computation.9 | loop fusion | flops 8257536 | bytes 18350080 | tf_op jit(solution)/shard_map/sub | solution.py:15
  307.5 8.6 %bitcast_multiply_fusion = f32[16,3,16,7168]{3,2,1,0:T(8,128)} fusion(f32[16]{0:T(128)S(1)} %mul.95, f32[4,1,16,7168]{3,2,0,1:T(8,128)S(1)} %bitcast.19, f32[4,1,16,7168]{3,2,0,1:T(8,128)S(1)} %bitcast.18, f32[4,1,16,7168]{3,2,0,1:T(8,128)S(1)} %bitcast.17), kind=kLoop, calls=%fused_computation | loop fusion | flops 8257536 | bytes 27525184 | tf_op jit(solution)/shard_map/mul | solution.py:35
  316.1 0.0 reduce-scatter.5.cloned.1.call-update
  316.1 174.2 %reduce-scatter.5.cloned.1.call-done = f32[1,3,16,7168]{3,2,1,0:T(8,128)} async-done(((f32[16,3,16,7168]{3,2,1,0:T(8,128)}), f32[1,3,16,7168]{3,2,1,0:T(8,128)}) %reduce-scatter.5.cloned.1.call-update) | async-done | bytes 1376272 | tf_op jit(solution)/shard_map/reduce_scatter | solution.py:36
Async XLA Ops:
  7.2 0.8 copy-start
  7.2 294.2 %copy-start.1 = (f32[1,64,7168]{2,1,0:T(8,128)S(1)}, f32[1,64,7168]{2,1,0:T(8,128)}, u32[]{:S(2)}) copy-start(f32[1,64,7168]{2,1,0:T(8,128)} %param.6) | copy-start | bytes 5505028
  7.2 294.2 %reduce-scatter.3.cloned.1.call-start = ((), (), s32[]{:S(2)}) async-start(), calls=%async_computation.2 | async-start | bytes 16515072 | tf_op jit(solution)/shard_map/reduce_scatter | solution.py:8
  7.9 482.4 %reduce-scatter.5.cloned.1.call-start = ((), (), s32[]{:S(2)}) async-start(), calls=%async_computation.3 | async-start | bytes 23396352 | tf_op jit(solution)/shard_map/reduce_scatter | solution.py:36
Sparse Core Ops, SparseCore 0:
  10.4 290.8 reduce-scatter.2
  316.3 173.9 reduce-scatter.4
where the time goes:
time: 497 us
  waiting for transfers between devices  468 us (94%)
  other arithmetic  14.8 us (3%)
  between operations  14.1 us (3%)
    reduce_scatter x1, waiting for transfers between devices, per_device(): grad = lax.psum_scatter(grad_parts, 'dp', scatter_dimension=2, tiled=True)  293 us
    reduce_scatter x1, waiting for transfers between devices, per_device(): owned = lax.psum_scatter(weighted, 'rec', scatter_dimension=0, tiled=True)  174 us
  transfers between devices with their start and end apart: 2, of which 2 were waited for; matrix products, arithmetic and copies ran while one was open for 0% of the time, Pallas kernels for 0%

commit v1 on v0

v1 whole, which is shorter than its diff:
```python
import functools

import jax
import jax.numpy as jnp
from jax import lax
from jax.experimental import pallas as pl
from jax.experimental.pallas import tpu as pltpu
from jax.sharding import PartitionSpec as P

MESH = pl.DeviceIdType.MESH
WIDTH = 256
AHEAD = 3

RELAY_UP, RELAY_DOWN, DIRECT_UP, DIRECT_DOWN, SECOND_UP, SECOND_DOWN = range(6)
ZL, CORE, X, ZH = 6, 7, 8, 14
SLOTS = 15


def kernel(
    chunks, width,
    g_ref, p_ref, m_ref, v_ref, gen_ref,
    np_ref, nm_ref, nv_ref, par_ref,
    own, up, down, yr, zr, pmv, dif, cr, wgt, xr, hr,
    ssem, rsem, lsem, osem,
):
    dp = lax.axis_index("dp")
    rec = lax.axis_index("rec")
    y, zl = dp // 2, dp % 2
    x, zh, core = rec // 4, (rec // 2) % 2, rec % 2
    y_up, y_down, y_far = (y + 1) % 4, (y + 3) % 4, (y + 2) % 4
    x_up, x_down, x_far = (x + 1) % 4, (x + 3) % 4, (x + 2) % 4
    to_y_up = (y_up * 2 + zl, rec)
    to_y_down = (y_down * 2 + zl, rec)
    to_zl = (y * 2 + 1 - zl, rec)
    to_core = (dp, x * 4 + zh * 2 + 1 - core)
    to_zh = (dp, x * 4 + (1 - zh) * 2 + core)
    to_x_up = (dp, x_up * 4 + zh * 2 + core)
    to_x_down = (dp, x_down * 4 + zh * 2 + core)

    barrier = pltpu.get_barrier_semaphore()
    peers = (to_y_up, to_y_down, to_zl, to_core, to_zh, to_x_up, to_x_down)
    for peer in peers:
        pl.semaphore_signal(barrier, inc=1, device_id=peer, device_id_type=MESH)
    pl.semaphore_wait(barrier, len(peers))

    def cols(k):
        return pl.ds(pl.multiple_of(k * width, width), width)

    def remote(k, slot, src, dst, device):
        return pltpu.make_async_remote_copy(
            src_ref=src, dst_ref=dst, send_sem=ssem.at[k, slot], recv_sem=rsem.at[k, slot],
            device_id=device, device_id_type=MESH,
        )

    def y_copy(k, slot):
        def rows(block, half):
            return g_ref.at[0, 0, pl.ds(pl.multiple_of(block * 128 + half * 64, 64), 64), cols(k)]

        src = {
            RELAY_UP: lambda: rows(y_far, 0),
            RELAY_DOWN: lambda: rows(y_far, 1),
            DIRECT_UP: lambda: rows(y_up, 1),
            DIRECT_DOWN: lambda: rows(y_down, 0),
            SECOND_UP: lambda: yr.at[k, RELAY_UP],
            SECOND_DOWN: lambda: yr.at[k, RELAY_DOWN],
        }[slot]()
        return remote(k, slot, src, yr.at[k, slot], to_y_up if slot % 2 == 0 else to_y_down)

    def x_copy(k, slot):
        src = {
            RELAY_UP: lambda: wgt.at[k, x_far, 0],
            RELAY_DOWN: lambda: wgt.at[k, x_far, 1],
            DIRECT_UP: lambda: wgt.at[k, x_up, 1],
            DIRECT_DOWN: lambda: wgt.at[k, x_down, 0],
            SECOND_UP: lambda: xr.at[k, RELAY_UP],
            SECOND_DOWN: lambda: xr.at[k, RELAY_DOWN],
        }[slot]()
        return remote(k, X + slot, src, xr.at[k, slot], to_x_up if slot % 2 == 0 else to_x_down)

    def zl_copy(k):
        return remote(k, ZL, own.at[k, 1 - zl], zr.at[k], to_zl)

    def core_copy(k):
        return remote(k, CORE, dif.at[k, 1 - core], cr.at[k], to_core)

    def zh_copy(k):
        return remote(k, ZH, wgt.at[k, x, 1 - zh], hr.at[k], to_zh)

    def recv_done(k, slot, buf):
        remote(k, slot, buf, buf, to_core).wait_recv()

    def load(k, i):
        def rows(block, half, n):
            return g_ref.at[0, 0, pl.ds(pl.multiple_of(block * 128 + half * 64, 64), n), cols(k)]

        src, dst = (
            lambda: (rows(y_up, 0, 64), up.at[k]),
            lambda: (rows(y_down, 1, 64), down.at[k]),
            lambda: (rows(y, 0, 64), own.at[k, 0]),
            lambda: (rows(y, 1, 64), own.at[k, 1]),
            lambda: (p_ref.at[0, :, cols(k)], pmv.at[k, 0]),
            lambda: (m_ref.at[0, :, cols(k)], pmv.at[k, 1]),
            lambda: (v_ref.at[0, :, cols(k)], pmv.at[k, 2]),
        )[i]()
        return pltpu.make_async_copy(src, dst, lsem.at[k, i])

    def store(k, i):
        src, dst = (
            lambda: (pmv.at[k, 0], np_ref.at[0, :, cols(k)]),
            lambda: (pmv.at[k, 1], nm_ref.at[0, :, cols(k)]),
            lambda: (pmv.at[k, 2], nv_ref.at[0, :, cols(k)]),
            lambda: (wgt.at[k, x, zh], par_ref.at[0, 0, :, :, cols(k)]),
        )[i]()
        return pltpu.make_async_copy(src, dst, osem.at[k, i])

    def begin(k):
        for slot in (RELAY_UP, RELAY_DOWN, DIRECT_UP, DIRECT_DOWN):
            y_copy(k, slot).start()
        for i in range(7):
            load(k, i).start()

    def y_relay(k):
        for slot, mine, i, onward in ((RELAY_UP, up, 0, SECOND_UP), (RELAY_DOWN, down, 1, SECOND_DOWN)):
            load(k, i).wait()
            recv_done(k, slot, yr.at[k, slot])
            yr[k, slot] = yr[k, slot] + mine[k]
            y_copy(k, onward).start()

    def y_half(k, half):
        pltpu.make_async_copy(own.at[k, half], own.at[k, half], lsem.at[k, 2 + half]).wait()
        recv_done(k, 3 - half, yr.at[k, 3 - half])
        recv_done(k, 4 + half, yr.at[k, 4 + half])
        own[k, half] = own[k, half] + yr[k, 3 - half] + yr[k, 4 + half]

    def y_final(k):
        y_half(k, 1 - zl)
        zl_copy(k).start()
        y_half(k, zl)

    def adam(k):
        for i in (4, 5, 6):
            load(k, i).wait()
        recv_done(k, ZL, zr.at[k])
        bias_one = 1.0 - 0.9**10
        bias_two = 1.0 - 0.999**10
        for q in range(4):
            r = pl.ds(q * 16, 16)
            grad = own[k, zl, r] + zr[k, r]
            params, first, second = pmv[k, 0, r], pmv[k, 1, r], pmv[k, 2, r]
            square = grad * grad
            new_first = 0.9 * first + 0.1 * grad
            new_second = 0.999 * second + 0.001 * square
            step = new_first / bias_one / (jnp.sqrt(new_second / bias_two) + 1e-08) + 0.1 * params
            dif[k, q % 2, q // 2, 0] = step
            dif[k, q % 2, q // 2, 1] = grad - first
            dif[k, q % 2, q // 2, 2] = square - second
            pmv[k, 0, r] = params - 0.001 * step
            pmv[k, 1, r] = new_first
            pmv[k, 2, r] = new_second
        core_copy(k).start()
        for i in range(3):
            store(k, i).start()

    def weigh(k):
        recv_done(k, CORE, cr.at[k])
        for half in range(2):
            mine = dif[k, core, half]
            other = cr[k, half]
            for j in range(4):
                a = gen_ref[j, rec]
                b = gen_ref[j, rec + 1 - 2 * core]
                wgt[k, j, half] = a * mine + b * other
        for slot in (RELAY_UP, RELAY_DOWN, DIRECT_UP, DIRECT_DOWN):
            x_copy(k, slot).start()

    def x_relay(k):
        for slot, block, half, onward in ((RELAY_UP, x_up, 0, SECOND_UP), (RELAY_DOWN, x_down, 1, SECOND_DOWN)):
            recv_done(k, X + slot, xr.at[k, slot])
            xr[k, slot] = xr[k, slot] + wgt[k, block, half]
            x_copy(k, onward).start()

    def x_half(k, half):
        recv_done(k, X + 3 - half, xr.at[k, 3 - half])
        recv_done(k, X + 4 + half, xr.at[k, 4 + half])
        wgt[k, x, half] = wgt[k, x, half] + xr[k, 3 - half] + xr[k, 4 + half]

    def x_final(k):
        x_half(k, 1 - zh)
        zh_copy(k).start()
        x_half(k, zh)

    def finish(k):
        recv_done(k, ZH, hr.at[k])
        wgt[k, x, zh] = wgt[k, x, zh] + hr[k]
        store(k, 3).start()

    for k in range(AHEAD):
        begin(k)

    stages = (y_relay, y_final, adam, weigh, x_relay, x_final, finish)

    def body(t, carry):
        @pl.when(t + AHEAD < chunks)
        def _():
            begin(t + AHEAD)

        for lag, stage in enumerate(stages):
            @pl.when(jnp.logical_and(t >= lag, t - lag < chunks))
            def _(stage=stage, lag=lag):
                stage(t - lag)

        return carry

    lax.fori_loop(0, chunks + len(stages) - 1, body, 0)

    def drain(k, carry):
        for slot in range(6):
            y_copy(k, slot).wait_send()
            x_copy(k, slot).wait_send()
        zl_copy(k).wait_send()
        core_copy(k).wait_send()
        zh_copy(k).wait_send()
        for i in range(4):
            store(k, i).wait()
        return carry

    lax.fori_loop(0, chunks, drain, 0)


def per_device(grad_parts, params, first_moment, second_moment, generator):
    width_all = params.shape[2]
    width = WIDTH
    chunks = width_all // width
    any_spec = pl.BlockSpec(memory_space=pl.ANY)
    f32 = jnp.float32
    return pl.pallas_call(
        functools.partial(kernel, chunks, width),
        out_shape=(
            jax.ShapeDtypeStruct(params.shape, f32),
            jax.ShapeDtypeStruct(params.shape, f32),
            jax.ShapeDtypeStruct(params.shape, f32),
            jax.ShapeDtypeStruct((1, 1, 3, 16, width_all), f32),
        ),
        in_specs=[any_spec] * 4 + [pl.BlockSpec(memory_space=pltpu.SMEM)],
        out_specs=(any_spec,) * 4,
        scratch_shapes=[
            pltpu.VMEM((chunks, 2, 64, width), f32),
            pltpu.VMEM((chunks, 64, width), f32),
            pltpu.VMEM((chunks, 64, width), f32),
            pltpu.VMEM((chunks, 6, 64, width), f32),
            pltpu.VMEM((chunks, 64, width), f32),
            pltpu.VMEM((chunks, 3, 64, width), f32),
            pltpu.VMEM((chunks, 2, 2, 3, 16, width), f32),
            pltpu.VMEM((chunks, 2, 3, 16, width), f32),
            pltpu.VMEM((chunks, 4, 2, 3, 16, width), f32),
            pltpu.VMEM((chunks, 6, 3, 16, width), f32),
            pltpu.VMEM((chunks, 3, 16, width), f32),
            pltpu.SemaphoreType.DMA((chunks, SLOTS)),
            pltpu.SemaphoreType.DMA((chunks, SLOTS)),
            pltpu.SemaphoreType.DMA((chunks, 7)),
            pltpu.SemaphoreType.DMA((chunks, 4)),
        ],
        compiler_params=pltpu.CompilerParams(
            collective_id=0, has_side_effects=True, vmem_limit_bytes=60 << 20
        ),
        cost_estimate=pl.CostEstimate(
            flops=100_000_000, bytes_accessed=60_000_000, transcendentals=458_752
        ),
    )(grad_parts, params, first_moment, second_moment, generator)


def solution(mesh):
    in_specs = (
        P("dp", "rec", None, None),
        P("rec", "dp", None),
        P("rec", "dp", None),
        P("rec", "dp", None),
        P(),
    )
    out_specs = (
        P("rec", "dp", None),
        P("rec", "dp", None),
        P("rec", "dp", None),
        P("dp", "rec", None, None, None),
    )
    return jax.shard_map(
        per_device, mesh=mesh, in_specs=in_specs, out_specs=out_specs, check_vma=False
    )
```

time: 497 us -> 177 us (0.36)
  waiting for transfers between devices: 468 us -> 0 us
  Pallas kernels: 0 us -> 165 us
  other arithmetic: 14.8 us -> 0 us
  between operations: 14.1 us -> 0.65 us
  local copies, waits for them, and re-layouts: 0.36 us -> 8.24 us
    reduce_scatter x2 -> x0, waiting for transfers between devices: 467 us -> none  [the longest x1 293 us: per_device(): grad = lax.psum_scatter(grad_parts, 'dp', scatter_dimension=2, tiled=True)]
    pallas_call x0 -> x1, Pallas kernels: none -> 165 us  [per_device(): pl.pallas_call(functools.partial(kernel, chunks, width), out_shape=(jax.S...]
    mul x1 -> x0, other arithmetic: 8.59 us -> none  [per_device(): weighted = (column * stacked[None]).reshape(members, 3, piece_rows, width)]
    unnamed x4 -> x10, local copies, waits for them, and re-layouts: 0.01 us -> 8.24 us
    sub x1 -> x0, other arithmetic: 6.17 us -> none  [per_device(): new_params = params - 0.001 * step_dir]
  transfers between devices with their start and end apart: 2 -> 0, of which waited for: 2 -> 0; matrix products, arithmetic and copies ran while one was open for 0% -> 0% of each run, Pallas kernels for 0% -> 0%
where the time goes in v1:
time: 177 us; the launch traced here: 174 us
  Pallas kernels  165 us (93%)
  local copies, waits for them, and re-layouts  8.24 us (5%)
    pallas_call x1, Pallas kernels, per_device(): pl.pallas_call(functools.partial(kernel, chunks, width), out_shape=(jax.S...  165 us
    unnamed x10, local copies, waits for them, and re-layouts  8.24 us

profile of v1, /device:TPU:1, one launch (start us, length us, event | category | flops | bytes accessed | tf_op | source)
XLA Modules:
  0.0 174.0 jit_solution(12565783780186043619)
XLA Ops:
  0.6 165.1 %shard_map.84 = (f32[1,64,7168]{2,1,0:T(8,128)}, f32[1,64,7168]{2,1,0:T(8,128)}, f32[1,64,7168]{2,1,0:T(8,128)}, f32[1,1,3,16,7168]{4,3,2,1,0:T(8,128)}) custom-call(f32[1,1,512,7168]{3,2,1,0:T(8,128)} %g_ref.1, f32[1,64,7168]{2,1,0:T(8,128)} %p_ref.1, f32[1,64,7168]{2,1,0:T(8,128)} %m_ref.1, f32[1,64,7168]{2,1,0:T(8,128)} %v_ref.1, f32[4,16]{1,0:T(4,128)} %gen_ref.1), custom_call_target="tpu_custom_call" | custom-call | flops 100000000 | bytes 60000000 | tf_op jit(solution)/shard_map/pallas_call | solution.py:236
  165.8 0.0 copy-start.1
  165.8 3.0 %copy.13 = f32[1,64,7168]{2,1,0:T(8,128)} copy(f32[1,64,7168]{2,1,0:T(8,128)} %get-tuple-element.8) | data formatting | bytes 3670016
  168.8 0.0 copy-done.1
  168.8 0.0 copy-start
  168.8 1.2 copy.14
  170.0 0.9 copy-done
  170.9 0.0 copy-start.2
  170.9 1.2 copy.15
  172.2 0.8 copy-done.2
  172.9 1.1 copy.16
Async XLA Ops:
  165.8 3.0 %copy-start.1 = (f32[1,64,7168]{2,1,0:T(8,128)S(1)}, f32[1,64,7168]{2,1,0:T(8,128)}, u32[]{:S(2)}) copy-start(f32[1,64,7168]{2,1,0:T(8,128)} %get-tuple-element.9) | copy-start | bytes 5505028
  168.8 2.2 %copy-start = (f32[1,64,7168]{2,1,0:T(8,128)S(1)}, f32[1,64,7168]{2,1,0:T(8,128)}, u32[]{:S(2)}) copy-start(f32[1,64,7168]{2,1,0:T(8,128)} %get-tuple-element.10) | copy-start | bytes 5505028
  170.9 2.0 %copy-start.2 = (f32[1,1,3,16,7168]{4,3,2,1,0:T(8,128)S(1)}, f32[1,1,3,16,7168]{4,3,2,1,0:T(8,128)}, u32[]{:S(2)}) copy-start(f32[1,1,3,16,7168]{4,3,2,1,0:T(8,128)} %get-tuple-element.11) | copy-start | bytes 4128772

commit v2 on v0

v2 whole, which is shorter than its diff:
```python
import functools

import jax
import jax.numpy as jnp
from jax import lax
from jax.experimental import pallas as pl
from jax.experimental.pallas import tpu as pltpu
from jax.sharding import PartitionSpec as P

MESH = pl.DeviceIdType.MESH
TILE = 128

CHUNKS = (
    (True, False, 6), (True, False, 6), (False, False, 6), (False, False, 6), (False, False, 2),
    (False, False, 5), (False, False, 5), (False, False, 5), (False, False, 5), (False, False, 3),
    (False, False, 1), (False, False, 2), (False, False, 2), (False, False, 1), (False, False, 1),
)
BEGIN, ZSUM, YRELAY, YFINAL, ADAM, WEIGH, XRELAY, XFINAL, FINISH = range(9)
ORDER = (
    (BEGIN, 0), (BEGIN, 2), (YRELAY, 2), (BEGIN, 3), (YFINAL, 2), (ZSUM, 0),
    (YRELAY, 3), (BEGIN, 1), (ADAM, 2), (YRELAY, 0), (WEIGH, 2), (BEGIN, 4),
    (XRELAY, 2), (YFINAL, 3), (BEGIN, 5), (ADAM, 0), (YRELAY, 4), (WEIGH, 0),
    (XFINAL, 2), (ZSUM, 1), (YRELAY, 5), (XRELAY, 0), (ADAM, 3), (YFINAL, 4),
    (WEIGH, 3), (YRELAY, 1), (XFINAL, 0), (FINISH, 2), (ADAM, 4), (BEGIN, 6),
    (XRELAY, 3), (YFINAL, 5), (WEIGH, 4), (ADAM, 1), (WEIGH, 1), (XFINAL, 3),
    (YRELAY, 6), (FINISH, 0), (XRELAY, 4), (ADAM, 5), (BEGIN, 7), (XRELAY, 1),
    (WEIGH, 5), (YFINAL, 6), (XFINAL, 4), (FINISH, 3), (YRELAY, 7), (XFINAL, 1),
    (ADAM, 6), (BEGIN, 8), (XRELAY, 5), (WEIGH, 6), (FINISH, 4), (YFINAL, 7),
    (XFINAL, 5), (YRELAY, 8), (FINISH, 1), (XRELAY, 6), (BEGIN, 9), (ADAM, 7),
    (WEIGH, 7), (YFINAL, 8), (XFINAL, 6), (BEGIN, 10), (YRELAY, 9), (FINISH, 5),
    (BEGIN, 11), (XRELAY, 7), (YRELAY, 10), (ADAM, 8), (YFINAL, 9), (BEGIN, 12),
    (WEIGH, 8), (YRELAY, 11), (XFINAL, 7), (YFINAL, 10), (FINISH, 6), (BEGIN, 13),
    (YRELAY, 12), (ADAM, 9), (XRELAY, 8), (BEGIN, 14), (WEIGH, 9), (YFINAL, 11),
    (YRELAY, 13), (YFINAL, 12), (XFINAL, 8), (YRELAY, 14), (FINISH, 7), (ADAM, 10),
    (XRELAY, 9), (YFINAL, 13), (ADAM, 11), (WEIGH, 10), (YFINAL, 14), (ADAM, 12),
    (WEIGH, 11), (WEIGH, 12), (XFINAL, 9), (XRELAY, 10), (XRELAY, 11), (FINISH, 8),
    (ADAM, 13), (XRELAY, 12), (ADAM, 14), (WEIGH, 13), (XFINAL, 10), (WEIGH, 14),
    (XFINAL, 11), (XFINAL, 12), (XRELAY, 13), (FINISH, 9), (XRELAY, 14), (FINISH, 10),
    (XFINAL, 13), (FINISH, 11), (XFINAL, 14), (FINISH, 12), (FINISH, 13), (FINISH, 14),
)

RELAY_UP, RELAY_DOWN, DIRECT_UP, DIRECT_DOWN, SECOND_UP, SECOND_DOWN = range(6)
Z_LO, CORE, X_RING, Z_HI, Z_HI_CORE = 6, 7, 8, 14, 15
SLOTS = 16
LOADS = 6


def kernel(
    g_ref, p_ref, m_ref, v_ref, gen_ref,
    np_ref, nm_ref, nv_ref, par_ref,
    own, got, dif, cr, wgt, xr, hr,
    ssem, rsem, lsem,
):
    dp = lax.axis_index("dp")
    rec = lax.axis_index("rec")
    y, zl = dp // 2, dp % 2
    x, zh, core = rec // 4, (rec // 2) % 2, rec % 2
    y_up, y_down, y_far = (y + 1) % 4, (y + 3) % 4, (y + 2) % 4
    x_up, x_down, x_far = (x + 1) % 4, (x + 3) % 4, (x + 2) % 4
    to_y_up = (y_up * 2 + zl, rec)
    to_y_down = (y_down * 2 + zl, rec)
    to_zl = (y * 2 + 1 - zl, rec)
    rec_core = x * 4 + zh * 2 + 1 - core
    rec_zh = x * 4 + (1 - zh) * 2 + core
    rec_both = x * 4 + (1 - zh) * 2 + 1 - core
    to_core, to_zh, to_both = (dp, rec_core), (dp, rec_zh), (dp, rec_both)
    to_x_up = (dp, x_up * 4 + zh * 2 + core)
    to_x_down = (dp, x_down * 4 + zh * 2 + core)

    barrier = pltpu.get_barrier_semaphore()
    peers = (to_y_up, to_y_down, to_zl, to_core, to_zh, to_both, to_x_up, to_x_down)
    for peer in peers:
        pl.semaphore_signal(barrier, inc=1, device_id=peer, device_id_type=MESH)
    pl.semaphore_wait(barrier, len(peers))

    starts = []
    for _, _, tiles in CHUNKS:
        starts.append(starts[-1] + last if starts else 0)
        last = tiles * TILE

    def cols(k):
        return pl.ds(starts[k], CHUNKS[k][2] * TILE)

    def over_cols(k, work):
        start, tiles = starts[k], CHUNKS[k][2]
        step = 2 * TILE if tiles % 2 == 0 else TILE
        n = tiles * TILE // step
        if n == 1:
            work(pl.ds(start, step))
        else:
            def body(i, carry):
                work(pl.ds(pl.multiple_of(start + i * step, TILE), step))
                return carry

            lax.fori_loop(0, n, body, 0)

    def remote(k, slot, src, dst, device):
        return pltpu.make_async_remote_copy(
            src_ref=src, dst_ref=dst, send_sem=ssem.at[k, slot], recv_sem=rsem.at[k, slot],
            device_id=device, device_id_type=MESH,
        )

    def z_first(k):
        return CHUNKS[k][0]

    def early(k):
        return CHUNKS[k][1]

    def y_place(k, slot):
        return (4 + slot // 2, (slot % 2) * 32, 32) if z_first(k) else (slot, 0, 64)

    def y_in(k, slot):
        i, r, n = y_place(k, slot)
        return got.at[i, pl.ds(r, n), cols(k)]

    def y_copy(k, slot):
        def part(block, half):
            if z_first(k):
                return got.at[block, pl.ds(half * 32, 32), cols(k)]
            return g_ref.at[block, half, :, cols(k)]

        src = {
            RELAY_UP: lambda: part(y_far, 0),
            RELAY_DOWN: lambda: part(y_far, 1),
            DIRECT_UP: lambda: part(y_up, 1),
            DIRECT_DOWN: lambda: part(y_down, 0),
            SECOND_UP: lambda: y_in(k, RELAY_UP),
            SECOND_DOWN: lambda: y_in(k, RELAY_DOWN),
        }[slot]()
        return remote(k, slot, src, y_in(k, slot), to_y_up if slot % 2 == 0 else to_y_down)

    def zl_copy(k):
        if z_first(k):
            return remote(k, Z_LO, g_ref.at[:, 1 - zl, :, cols(k)], got.at[0:4, :, cols(k)], to_zl)
        return remote(k, Z_LO, own.at[1 - zl, :, cols(k)], got.at[6, :, cols(k)], to_zl)

    def group_copies(k):
        if early(k):
            return (
                remote(k, Z_HI_CORE, dif.at[1 - core, 1 - zh, :, :, cols(k)], cr.at[1, :, :, cols(k)], to_both),
                remote(k, Z_HI, dif.at[core, 1 - zh, :, :, cols(k)], hr.at[:, :, cols(k)], to_zh),
                remote(k, CORE, dif.at[1 - core, zh, :, :, cols(k)], cr.at[0, :, :, cols(k)], to_core),
            )
        return (remote(k, CORE, dif.at[1 - core, :, :, :, cols(k)], cr.at[:, :, :, cols(k)], to_core),)

    def x_part(k, block, half):
        if early(k):
            return wgt.at[block, 0, :, pl.ds(half * 8, 8), cols(k)]
        return wgt.at[block, half, :, :, cols(k)]

    def x_in(k, slot):
        return xr.at[slot, :, pl.ds(0, 8 if early(k) else 16), cols(k)]

    def x_copy(k, slot):
        src = {
            RELAY_UP: lambda: x_part(k, x_far, 0),
            RELAY_DOWN: lambda: x_part(k, x_far, 1),
            DIRECT_UP: lambda: x_part(k, x_up, 1),
            DIRECT_DOWN: lambda: x_part(k, x_down, 0),
            SECOND_UP: lambda: x_in(k, RELAY_UP),
            SECOND_DOWN: lambda: x_in(k, RELAY_DOWN),
        }[slot]()
        return remote(k, X_RING + slot, src, x_in(k, slot), to_x_up if slot % 2 == 0 else to_x_down)

    def zh_copy(k):
        return remote(k, Z_HI, wgt.at[x, 1 - zh, :, :, cols(k)], hr.at[:, :, cols(k)], to_zh)

    def arrived(k, slot, buf):
        remote(k, slot, buf, buf, to_core).wait_recv()

    def loads(k):
        c = cols(k)
        if z_first(k):
            pairs = [(g_ref.at[:, zl, :, c], own.at[:, :, c])]
        else:
            pairs = [
                (g_ref.at[y_up, 0, :, c], own.at[2, :, c]),
                (g_ref.at[y_down, 1, :, c], own.at[3, :, c]),
                (g_ref.at[y, :, :, c], own.at[0:2, :, c]),
            ]
        state = ((p_ref, np_ref), (m_ref, nm_ref), (v_ref, nv_ref))
        pairs += [(src.at[0, :, c], dst.at[0, :, c]) for src, dst in state]
        return [functools.partial(pltpu.make_async_copy, src, dst, lsem.at[k, i]) for i, (src, dst) in enumerate(pairs)]

    def begin(k):
        if z_first(k):
            zl_copy(k).start()
        else:
            for slot in (RELAY_UP, RELAY_DOWN, DIRECT_UP, DIRECT_DOWN):
                y_copy(k, slot).start()
        for copy in loads(k):
            copy().start()

    def zsum(k):
        loads(k)[0]().wait()
        arrived(k, Z_LO, got.at[0:4, :, cols(k)])

        def add(block):
            def work(c):
                got[block, :, c] = got[block, :, c] + own[block, :, c]

            over_cols(k, work)

        add(y_far)
        y_copy(k, RELAY_UP).start()
        y_copy(k, RELAY_DOWN).start()
        add(y_up)
        y_copy(k, DIRECT_UP).start()
        add(y_down)
        y_copy(k, DIRECT_DOWN).start()
        add(y)

    def yrelay(k):
        for slot, block, onward in ((RELAY_UP, y_up, SECOND_UP), (RELAY_DOWN, y_down, SECOND_DOWN)):
            if not z_first(k):
                loads(k)[slot]().wait()
            arrived(k, slot, y_in(k, slot))
            i, r, n = y_place(k, slot)

            def work(c):
                if z_first(k):
                    mine = got[block, pl.ds(slot * 32, 32), c]
                else:
                    mine = own[2 + slot, :, c]
                got[i, pl.ds(r, n), c] = got[i, pl.ds(r, n), c] + mine

            over_cols(k, work)
            y_copy(k, onward).start()

    def yfinal(k):
        loads(k)[2]().wait()
        for turn, half in enumerate((1 - zl, zl)):
            for slot in (3 - half, 4 + half):
                arrived(k, slot, got.at[slot, :, cols(k)])

            def work(c):
                own[half, :, c] = own[half, :, c] + got[3 - half, :, c] + got[4 + half, :, c]

            over_cols(k, work)
            if turn == 0:
                zl_copy(k).start()

    def adam(k):
        for copy in loads(k)[-3:]:
            copy().wait()
        if z_first(k):
            for slot in (DIRECT_DOWN, SECOND_UP, DIRECT_UP, SECOND_DOWN):
                arrived(k, slot, y_in(k, slot))
        else:
            arrived(k, Z_LO, got.at[6, :, cols(k)])
        bias_one = 1.0 - 0.9**10
        bias_two = 1.0 - 0.999**10

        def work(c):
            for q in range(4):
                r = pl.ds(q * 16, 16)
                if z_first(k):
                    grad = got[y, r, c]
                    for slot in ((DIRECT_DOWN, SECOND_UP) if q < 2 else (DIRECT_UP, SECOND_DOWN)):
                        i, first_row, _ = y_place(k, slot)
                        grad = grad + got[i, pl.ds(first_row + (q % 2) * 16, 16), c]
                else:
                    grad = own[zl, r, c] + got[6, r, c]
                params, first, second = np_ref[0, r, c], nm_ref[0, r, c], nv_ref[0, r, c]
                square = grad * grad
                new_first = 0.9 * first + 0.1 * grad
                new_second = 0.999 * second + 0.001 * square
                step = new_first / bias_one / (jnp.sqrt(new_second / bias_two) + 1e-08) + 0.1 * params
                dif[q % 2, q // 2, 0, :, c] = step
                dif[q % 2, q // 2, 1, :, c] = grad - first
                dif[q % 2, q // 2, 2, :, c] = square - second
                np_ref[0, r, c] = params - 0.001 * step
                nm_ref[0, r, c] = new_first
                nv_ref[0, r, c] = new_second

        over_cols(k, work)
        for copy in group_copies(k):
            copy.start()

    def weigh(k):
        if early(k):
            arrived(k, CORE, cr.at[0, :, :, cols(k)])
            arrived(k, Z_HI, hr.at[:, :, cols(k)])
            arrived(k, Z_HI_CORE, cr.at[1, :, :, cols(k)])
        else:
            arrived(k, CORE, cr.at[:, :, :, cols(k)])

        def work(c):
            if early(k):
                fields = (dif[core, zh, :, :, c], cr[0, :, :, c], hr[:, :, c], cr[1, :, :, c])
                for j in range(4):
                    total = gen_ref[j, rec] * fields[0]
                    for member, field in zip((rec_core, rec_zh, rec_both), fields[1:]):
                        total = total + gen_ref[j, member] * field
                    wgt[j, 0, :, :, c] = total
            else:
                for half in range(2):
                    mine, other = dif[core, half, :, :, c], cr[half, :, :, c]
                    for j in range(4):
                        wgt[j, half, :, :, c] = gen_ref[j, rec] * mine + gen_ref[j, rec_core] * other

        over_cols(k, work)
        for slot in (RELAY_UP, RELAY_DOWN, DIRECT_UP, DIRECT_DOWN):
            x_copy(k, slot).start()

    def xrelay(k):
        for slot, block, onward in ((RELAY_UP, x_up, SECOND_UP), (RELAY_DOWN, x_down, SECOND_DOWN)):
            arrived(k, X_RING + slot, x_in(k, slot))

            def work(c):
                if early(k):
                    r = pl.ds(0, 8)
                    xr[slot, :, r, c] = xr[slot, :, r, c] + wgt[block, 0, :, pl.ds(slot * 8, 8), c]
                else:
                    xr[slot, :, :, c] = xr[slot, :, :, c] + wgt[block, slot, :, :, c]

            over_cols(k, work)
            x_copy(k, onward).start()

    def xfinal(k):
        if early(k):
            for slot in (DIRECT_DOWN, SECOND_UP, DIRECT_UP, SECOND_DOWN):
                arrived(k, X_RING + slot, x_in(k, slot))

            def work(c):
                r = pl.ds(0, 8)
                for half in range(2):
                    h = pl.ds(half * 8, 8)
                    par_ref[0, 0, :, h, c] = wgt[x, 0, :, h, c] + xr[3 - half, :, r, c] + xr[4 + half, :, r, c]

            over_cols(k, work)
            return
        for turn, half in enumerate((1 - zh, zh)):
            for slot in (3 - half, 4 + half):
                arrived(k, X_RING + slot, xr.at[slot, :, :, cols(k)])

            def work(c):
                wgt[x, half, :, :, c] = wgt[x, half, :, :, c] + xr[3 - half, :, :, c] + xr[4 + half, :, :, c]

            over_cols(k, work)
            if turn == 0:
                zh_copy(k).start()

    def finish(k):
        arrived(k, Z_HI, hr.at[:, :, cols(k)])

        def work(c):
            par_ref[0, 0, :, :, c] = wgt[x, zh, :, :, c] + hr[:, :, c]

        over_cols(k, work)

    stages = {
        BEGIN: begin, ZSUM: zsum, YRELAY: yrelay, YFINAL: yfinal, ADAM: adam,
        WEIGH: weigh, XRELAY: xrelay, XFINAL: xfinal, FINISH: finish,
    }
    for stage, k in ORDER:
        stages[stage](k)

    for k in range(len(CHUNKS)):
        for slot in range(6):
            y_copy(k, slot).wait_send()
            x_copy(k, slot).wait_send()
        zl_copy(k).wait_send()
        for copy in group_copies(k):
            copy.wait_send()
        if not early(k):
            zh_copy(k).wait_send()


def copy_out(*refs):
    n = len(refs) // 2
    sems = refs[-1]
    copies = []
    for i in range(4):
        src, dst = refs[i], refs[4 + i]
        for part in range(4):
            if i < 3:
                where = (0, pl.ds(part * 16, 16))
            elif part < 3:
                where = (0, 0, part)
            else:
                continue
            copies.append(pltpu.make_async_copy(src.at[where], dst.at[where], sems.at[i, part]))
    for copy in copies:
        copy.start()
    for copy in copies:
        copy.wait()


def per_device(grad_parts, params, first_moment, second_moment, generator):
    width = params.shape[2]
    assert sum(tiles for _, _, tiles in CHUNKS) * TILE == width
    n = len(CHUNKS)
    any_spec = pl.BlockSpec(memory_space=pl.ANY)
    f32 = jnp.float32
    outs = (jax.ShapeDtypeStruct(params.shape, f32),) * 3 + (jax.ShapeDtypeStruct((1, 1, 3, 16, width), f32),)
    results = pl.pallas_call(
        kernel,
        out_shape=tuple(pltpu.VMEM(out.shape, out.dtype) for out in outs),
        in_specs=[any_spec] * 4 + [pl.BlockSpec(memory_space=pltpu.SMEM)],
        out_specs=(pl.BlockSpec(memory_space=pltpu.VMEM),) * 4,
        scratch_shapes=[
            pltpu.VMEM((4, 64, width), f32),
            pltpu.VMEM((7, 64, width), f32),
            pltpu.VMEM((2, 2, 3, 16, width), f32),
            pltpu.VMEM((2, 3, 16, width), f32),
            pltpu.VMEM((4, 2, 3, 16, width), f32),
            pltpu.VMEM((6, 3, 16, width), f32),
            pltpu.VMEM((3, 16, width), f32),
            pltpu.SemaphoreType.DMA((n, SLOTS)),
            pltpu.SemaphoreType.DMA((n, SLOTS)),
            pltpu.SemaphoreType.DMA((n, LOADS)),
        ],
        compiler_params=pltpu.CompilerParams(
            collective_id=0, has_side_effects=True, vmem_limit_bytes=50 << 20
        ),
        cost_estimate=pl.CostEstimate(
            flops=100_000_000, bytes_accessed=60_000_000, transcendentals=458_752
        ),
        name="adam_parity",
    )(grad_parts.reshape(4, 2, 64, width), params, first_moment, second_moment, generator)
    return pl.pallas_call(
        copy_out,
        out_shape=outs,
        in_specs=[any_spec] * 4,
        out_specs=(any_spec,) * 4,
        scratch_shapes=[pltpu.SemaphoreType.DMA((4, 4))],
        compiler_params=pltpu.CompilerParams(vmem_limit_bytes=1 << 20),
        cost_estimate=pl.CostEstimate(flops=0, bytes_accessed=13_800_000, transcendentals=0),
        name="copy_out",
    )(*results)


def solution(mesh):
    in_specs = (
        P("dp", "rec", None, None),
        P("rec", "dp", None),
        P("rec", "dp", None),
        P("rec", "dp", None),
        P(),
    )
    out_specs = (
        P("rec", "dp", None),
        P("rec", "dp", None),
        P("rec", "dp", None),
        P("dp", "rec", None, None, None),
    )
    return jax.shard_map(
        per_device, mesh=mesh, in_specs=in_specs, out_specs=out_specs, check_vma=False
    )
```

time: 497 us -> 144 us (0.29)
  waiting for transfers between devices: 468 us -> 0 us
  Pallas kernels: 0 us -> 141 us
  other arithmetic: 14.8 us -> 0 us
  between operations: 14.1 us -> 0.64 us
    reduce_scatter x2 -> x0, waiting for transfers between devices: 467 us -> none  [the longest x1 293 us: per_device(): grad = lax.psum_scatter(grad_parts, 'dp', scatter_dimension=2, tiled=True)]
    pallas_call x0 -> x2, Pallas kernels: none -> 141 us  [the longest x1 138 us: per_device(): pl.pallas_call(kernel, out_shape=tuple((pltpu.VMEM(out.shape, out.dtype)...]
    mul x1 -> x0, other arithmetic: 8.59 us -> none  [per_device(): weighted = (column * stacked[None]).reshape(members, 3, piece_rows, width)]
    sub x1 -> x0, other arithmetic: 6.17 us -> none  [per_device(): new_params = params - 0.001 * step_dir]
  transfers between devices with their start and end apart: 2 -> 0, of which waited for: 2 -> 0; matrix products, arithmetic and copies ran while one was open for 0% -> 0% of each run, Pallas kernels for 0% -> 0%
where the time goes in v2:
time: 144 us; the launch traced here: 142 us
  Pallas kernels  141 us (98%)
    pallas_call x1, Pallas kernels, per_device(): pl.pallas_call(kernel, out_shape=tuple((pltpu.VMEM(out.shape, out.dtype)...  138 us
    pallas_call x1, Pallas kernels, per_device(): pl.pallas_call(copy_out, out_shape=outs, in_specs=[any_spec] * 4, out_spe...  2.97 us

profile of v2, /device:TPU:1, one launch (start us, length us, event | category | flops | bytes accessed | tf_op | source)
XLA Modules:
  0.0 142.1 jit_solution(2667882705434320694)
XLA Ops:
  0.6 138.5 %adam_parity.1 = (f32[1,64,7168]{2,1,0:T(8,128)S(1)}, f32[1,64,7168]{2,1,0:T(8,128)S(1)}, f32[1,64,7168]{2,1,0:T(8,128)S(1)}, f32[1,1,3,16,7168]{4,3,2,1,0:T(8,128)S(1)}) custom-call(f32[4,2,64,7168]{3,2,1,0:T(8,128)} %bitcast.1, f32[1,64,7168]{2,1,0:T(8,128)} %p_ref.1, f32[1,64,7168]{2,1,0:T(8,128)} %m_ref.1, f32[1,64,7168]{2,1,0:T(8,128)} %v_ref.1, ...), custom_call_target="tpu_custom_call" | custom-call | flops 100000000 | bytes 60000000 | tf_op jit(solution)/shard_map/adam_parity/pallas_call | solution.py:397
  139.1 3.0 %copy_out.1 = (f32[1,64,7168]{2,1,0:T(8,128)}, f32[1,64,7168]{2,1,0:T(8,128)}, f32[1,64,7168]{2,1,0:T(8,128)}, f32[1,1,3,16,7168]{4,3,2,1,0:T(8,128)}) custom-call(f32[1,64,7168]{2,1,0:T(8,128)S(1)} %get-tuple-element.8.refs_0_, f32[1,64,7168]{2,1,0:T(8,128)S(1)} %get-tuple-element.9.refs_1_, f32[1,64,7168]{2,1,0:T(8,128)S(1)} %get-tuple-element.10.refs_2_, ...), custom_call_target="tpu_custom_call" | custom-call | bytes 13800000 | tf_op jit(solution)/shard_map/copy_out/pallas_call | solution.py:422

commit v3 on v2

--- a/solution.py
+++ b/solution.py
@@ -11,35 +11,35 @@
 TILE = 128
 
 CHUNKS = (
-    (True, False, 6), (True, False, 6), (False, False, 6), (False, False, 6), (False, False, 2),
-    (False, False, 5), (False, False, 5), (False, False, 5), (False, False, 5), (False, False, 3),
-    (False, False, 1), (False, False, 2), (False, False, 2), (False, False, 1), (False, False, 1),
+    (0, 0, 0, 6), (0, 0, 0, 7), (1, 0, 0, 8), (0, 0, 0, 1), (0, 0, 0, 6), (0, 0, 0, 6), (0, 1, 0, 3),
+    (0, 0, 0, 3), (1, 0, 0, 4), (0, 1, 0, 2), (0, 0, 0, 2), (0, 1, 0, 2), (1, 1, 0, 3), (1, 0, 0, 1),
+    (1, 1, 1, 2),
 )
 BEGIN, ZSUM, YRELAY, YFINAL, ADAM, WEIGH, XRELAY, XFINAL, FINISH = range(9)
 ORDER = (
-    (BEGIN, 0), (BEGIN, 2), (YRELAY, 2), (BEGIN, 3), (YFINAL, 2), (ZSUM, 0),
-    (YRELAY, 3), (BEGIN, 1), (ADAM, 2), (YRELAY, 0), (WEIGH, 2), (BEGIN, 4),
-    (XRELAY, 2), (YFINAL, 3), (BEGIN, 5), (ADAM, 0), (YRELAY, 4), (WEIGH, 0),
-    (XFINAL, 2), (ZSUM, 1), (YRELAY, 5), (XRELAY, 0), (ADAM, 3), (YFINAL, 4),
-    (WEIGH, 3), (YRELAY, 1), (XFINAL, 0), (FINISH, 2), (ADAM, 4), (BEGIN, 6),
-    (XRELAY, 3), (YFINAL, 5), (WEIGH, 4), (ADAM, 1), (WEIGH, 1), (XFINAL, 3),
-    (YRELAY, 6), (FINISH, 0), (XRELAY, 4), (ADAM, 5), (BEGIN, 7), (XRELAY, 1),
-    (WEIGH, 5), (YFINAL, 6), (XFINAL, 4), (FINISH, 3), (YRELAY, 7), (XFINAL, 1),
-    (ADAM, 6), (BEGIN, 8), (XRELAY, 5), (WEIGH, 6), (FINISH, 4), (YFINAL, 7),
-    (XFINAL, 5), (YRELAY, 8), (FINISH, 1), (XRELAY, 6), (BEGIN, 9), (ADAM, 7),
-    (WEIGH, 7), (YFINAL, 8), (XFINAL, 6), (BEGIN, 10), (YRELAY, 9), (FINISH, 5),
-    (BEGIN, 11), (XRELAY, 7), (YRELAY, 10), (ADAM, 8), (YFINAL, 9), (BEGIN, 12),
-    (WEIGH, 8), (YRELAY, 11), (XFINAL, 7), (YFINAL, 10), (FINISH, 6), (BEGIN, 13),
-    (YRELAY, 12), (ADAM, 9), (XRELAY, 8), (BEGIN, 14), (WEIGH, 9), (YFINAL, 11),
-    (YRELAY, 13), (YFINAL, 12), (XFINAL, 8), (YRELAY, 14), (FINISH, 7), (ADAM, 10),
-    (XRELAY, 9), (YFINAL, 13), (ADAM, 11), (WEIGH, 10), (YFINAL, 14), (ADAM, 12),
-    (WEIGH, 11), (WEIGH, 12), (XFINAL, 9), (XRELAY, 10), (XRELAY, 11), (FINISH, 8),
-    (ADAM, 13), (XRELAY, 12), (ADAM, 14), (WEIGH, 13), (XFINAL, 10), (WEIGH, 14),
-    (XFINAL, 11), (XFINAL, 12), (XRELAY, 13), (FINISH, 9), (XRELAY, 14), (FINISH, 10),
-    (XFINAL, 13), (FINISH, 11), (XFINAL, 14), (FINISH, 12), (FINISH, 13), (FINISH, 14),
+    (BEGIN, 2), (BEGIN, 0), (YRELAY, 0), (BEGIN, 1), (YFINAL, 0), (YRELAY, 1),
+    (BEGIN, 8), (ZSUM, 2), (ADAM, 0), (YFINAL, 1), (BEGIN, 3), (WEIGH, 0),
+    (YRELAY, 2), (YRELAY, 3), (BEGIN, 4), (XRELAY, 0), (ADAM, 2), (BEGIN, 12),
+    (YFINAL, 3), (WEIGH, 2), (ADAM, 1), (YRELAY, 4), (XFINAL, 0), (WEIGH, 1),
+    (BEGIN, 5), (XRELAY, 2), (BEGIN, 13), (YFINAL, 4), (ADAM, 3), (WEIGH, 3),
+    (YRELAY, 5), (FINISH, 0), (XRELAY, 1), (BEGIN, 14), (BEGIN, 6), (ADAM, 4),
+    (YFINAL, 5), (BEGIN, 7), (XFINAL, 2), (WEIGH, 4), (YRELAY, 6), (XRELAY, 3),
+    (YRELAY, 7), (XFINAL, 1), (ADAM, 5), (ZSUM, 8), (XRELAY, 4), (YFINAL, 6),
+    (WEIGH, 5), (BEGIN, 9), (FINISH, 2), (YFINAL, 7), (XFINAL, 3), (YRELAY, 8),
+    (FINISH, 1), (XFINAL, 4), (BEGIN, 10), (YRELAY, 9), (ADAM, 6), (XRELAY, 5),
+    (ADAM, 8), (ADAM, 7), (BEGIN, 11), (FINISH, 3), (YRELAY, 10), (WEIGH, 8),
+    (WEIGH, 7), (YFINAL, 9), (FINISH, 4), (ZSUM, 12), (YRELAY, 11), (XFINAL, 5),
+    (WEIGH, 6), (XRELAY, 8), (YFINAL, 10), (ADAM, 9), (ZSUM, 13), (YRELAY, 12),
+    (ZSUM, 14), (YFINAL, 11), (XRELAY, 7), (YRELAY, 13), (FINISH, 5), (ADAM, 10),
+    (ADAM, 12), (XRELAY, 6), (WEIGH, 10), (WEIGH, 9), (ADAM, 13), (ADAM, 11),
+    (ADAM, 14), (XFINAL, 8), (XFINAL, 7), (WEIGH, 13), (XFINAL, 6), (XRELAY, 10),
+    (WEIGH, 12), (XRELAY, 9), (XRELAY, 13), (WEIGH, 11), (XFINAL, 10), (XRELAY, 12),
+    (WEIGH, 14), (XFINAL, 9), (FINISH, 8), (XFINAL, 13), (XRELAY, 11), (FINISH, 7),
+    (XFINAL, 12), (FINISH, 10), (FINISH, 13), (XFINAL, 11), (XFINAL, 14),
 )
 
 RELAY_UP, RELAY_DOWN, DIRECT_UP, DIRECT_DOWN, SECOND_UP, SECOND_DOWN = range(6)
+TO_UP, TO_DOWN, TO_FAR = range(3)
 Z_LO, CORE, X_RING, Z_HI, Z_HI_CORE = 6, 7, 8, 14, 15
 SLOTS = 16
 LOADS = 6
@@ -59,6 +59,7 @@
     x_up, x_down, x_far = (x + 1) % 4, (x + 3) % 4, (x + 2) % 4
     to_y_up = (y_up * 2 + zl, rec)
     to_y_down = (y_down * 2 + zl, rec)
+    to_y_far = (y_far * 2 + zl, rec)
     to_zl = (y * 2 + 1 - zl, rec)
     rec_core = x * 4 + zh * 2 + 1 - core
     rec_zh = x * 4 + (1 - zh) * 2 + core
@@ -67,22 +68,24 @@
     to_x_up = (dp, x_up * 4 + zh * 2 + core)
     to_x_down = (dp, x_down * 4 + zh * 2 + core)
 
+    to_x_far = (dp, x_far * 4 + zh * 2 + core)
+
     barrier = pltpu.get_barrier_semaphore()
-    peers = (to_y_up, to_y_down, to_zl, to_core, to_zh, to_both, to_x_up, to_x_down)
+    peers = (to_y_up, to_y_down, to_y_far, to_zl, to_core, to_zh, to_both, to_x_up, to_x_down, to_x_far)
     for peer in peers:
         pl.semaphore_signal(barrier, inc=1, device_id=peer, device_id_type=MESH)
     pl.semaphore_wait(barrier, len(peers))
 
     starts = []
-    for _, _, tiles in CHUNKS:
+    for _, _, _, tiles in CHUNKS:
         starts.append(starts[-1] + last if starts else 0)
         last = tiles * TILE
 
     def cols(k):
-        return pl.ds(starts[k], CHUNKS[k][2] * TILE)
+        return pl.ds(starts[k], CHUNKS[k][3] * TILE)
 
     def over_cols(k, work):
-        start, tiles = starts[k], CHUNKS[k][2]
+        start, tiles = starts[k], CHUNKS[k][3]
         step = 2 * TILE if tiles % 2 == 0 else TILE
         n = tiles * TILE // step
         if n == 1:
@@ -106,14 +109,27 @@
     def early(k):
         return CHUNKS[k][1]
 
+    def direct(k):
+        return CHUNKS[k][2]
+
+    def ring_slots(k):
+        return (TO_UP, TO_DOWN, TO_FAR) if direct(k) else (RELAY_UP, RELAY_DOWN, DIRECT_UP, DIRECT_DOWN)
+
     def y_place(k, slot):
         return (4 + slot // 2, (slot % 2) * 32, 32) if z_first(k) else (slot, 0, 64)
 
     def y_in(k, slot):
+        if direct(k):
+            return got.at[4 + slot, :, cols(k)] if z_first(k) else got.at[2 * slot:2 * slot + 2, :, cols(k)]
         i, r, n = y_place(k, slot)
         return got.at[i, pl.ds(r, n), cols(k)]
 
     def y_copy(k, slot):
+        if direct(k):
+            block = (y_up, y_down, y_far)[slot]
+            src = got.at[block, :, cols(k)] if z_first(k) else g_ref.at[block, :, :, cols(k)]
+            return remote(k, slot, src, y_in(k, slot), (to_y_up, to_y_down, to_y_far)[slot])
+
         def part(block, half):
             if z_first(k):
                 return got.at[block, pl.ds(half * 32, 32), cols(k)]
@@ -149,9 +165,16 @@
         return wgt.at[block, half, :, :, cols(k)]
 
     def x_in(k, slot):
+        if direct(k):
+            return xr.at[2 * slot, :, :, cols(k)] if early(k) else xr.at[2 * slot:2 * slot + 2, :, :, cols(k)]
         return xr.at[slot, :, pl.ds(0, 8 if early(k) else 16), cols(k)]
 
     def x_copy(k, slot):
+        if direct(k):
+            block = (x_up, x_down, x_far)[slot]
+            src = wgt.at[block, 0, :, :, cols(k)] if early(k) else wgt.at[block, :, :, :, cols(k)]
+            return remote(k, X_RING + slot, src, x_in(k, slot), (to_x_up, to_x_down, to_x_far)[slot])
+
         src = {
             RELAY_UP: lambda: x_part(k, x_far, 0),
             RELAY_DOWN: lambda: x_part(k, x_far, 1),
@@ -172,6 +195,8 @@
         c = cols(k)
         if z_first(k):
             pairs = [(g_ref.at[:, zl, :, c], own.at[:, :, c])]
+        elif direct(k):
+            pairs = [(g_ref.at[y, :, :, c], own.at[0:2, :, c])]
         else:
             pairs = [
                 (g_ref.at[y_up, 0, :, c], own.at[2, :, c]),
@@ -186,7 +211,7 @@
         if z_first(k):
             zl_copy(k).start()
         else:
-            for slot in (RELAY_UP, RELAY_DOWN, DIRECT_UP, DIRECT_DOWN):
+            for slot in ring_slots(k):
                 y_copy(k, slot).start()
         for copy in loads(k):
             copy().start()
@@ -201,13 +226,18 @@
 
             over_cols(k, work)
 
-        add(y_far)
-        y_copy(k, RELAY_UP).start()
-        y_copy(k, RELAY_DOWN).start()
-        add(y_up)
-        y_copy(k, DIRECT_UP).start()
-        add(y_down)
-        y_copy(k, DIRECT_DOWN).start()
+        if direct(k):
+            for slot, block in ((TO_FAR, y_far), (TO_UP, y_up), (TO_DOWN, y_down)):
+                add(block)
+                y_copy(k, slot).start()
+        else:
+            add(y_far)
+            y_copy(k, RELAY_UP).start()
+            y_copy(k, RELAY_DOWN).start()
+            add(y_up)
+            y_copy(k, DIRECT_UP).start()
+            add(y_down)
+            y_copy(k, DIRECT_DOWN).start()
         add(y)
 
     def yrelay(k):
@@ -228,13 +258,20 @@
             y_copy(k, onward).start()
 
     def yfinal(k):
-        loads(k)[2]().wait()
+        loads(k)[0 if direct(k) else 2]().wait()
+        if direct(k):
+            for slot in range(3):
+                arrived(k, slot, y_in(k, slot))
         for turn, half in enumerate((1 - zl, zl)):
-            for slot in (3 - half, 4 + half):
-                arrived(k, slot, got.at[slot, :, cols(k)])
+            if not direct(k):
+                for slot in (3 - half, 4 + half):
+                    arrived(k, slot, got.at[slot, :, cols(k)])
 
             def work(c):
-                own[half, :, c] = own[half, :, c] + got[3 - half, :, c] + got[4 + half, :, c]
+                if direct(k):
+                    own[half, :, c] = own[half, :, c] + got[half, :, c] + got[2 + half, :, c] + got[4 + half, :, c]
+                else:
+                    own[half, :, c] = own[half, :, c] + got[3 - half, :, c] + got[4 + half, :, c]
 
             over_cols(k, work)
             if turn == 0:
@@ -244,7 +281,7 @@
         for copy in loads(k)[-3:]:
             copy().wait()
         if z_first(k):
-            for slot in (DIRECT_DOWN, SECOND_UP, DIRECT_UP, SECOND_DOWN):
+            for slot in range(3) if direct(k) else (DIRECT_DOWN, SECOND_UP, DIRECT_UP, SECOND_DOWN):
                 arrived(k, slot, y_in(k, slot))
         else:
             arrived(k, Z_LO, got.at[6, :, cols(k)])
@@ -254,7 +291,9 @@
         def work(c):
             for q in range(4):
                 r = pl.ds(q * 16, 16)
-                if z_first(k):
+                if z_first(k) and direct(k):
+                    grad = got[y, r, c] + got[4, r, c] + got[5, r, c] + got[6, r, c]
+                elif z_first(k):
                     grad = got[y, r, c]
                     for slot in ((DIRECT_DOWN, SECOND_UP) if q < 2 else (DIRECT_UP, SECOND_DOWN)):
                         i, first_row, _ = y_place(k, slot)
@@ -300,7 +339,7 @@
                         wgt[j, half, :, :, c] = gen_ref[j, rec] * mine + gen_ref[j, rec_core] * other
 
         over_cols(k, work)
-        for slot in (RELAY_UP, RELAY_DOWN, DIRECT_UP, DIRECT_DOWN):
+        for slot in ring_slots(k):
             x_copy(k, slot).start()
 
     def xrelay(k):
@@ -318,6 +357,27 @@
             x_copy(k, onward).start()
 
     def xfinal(k):
+        if direct(k):
+            for slot in range(3):
+                arrived(k, X_RING + slot, x_in(k, slot))
+
+            def total(half, c):
+                return wgt[x, half, :, :, c] + xr[half, :, :, c] + xr[2 + half, :, :, c] + xr[4 + half, :, :, c]
+
+            if early(k):
+                def work(c):
+                    par_ref[0, 0, :, :, c] = total(0, c)
+
+                over_cols(k, work)
+                return
+            for turn, half in enumerate((1 - zh, zh)):
+                def work(c):
+                    wgt[x, half, :, :, c] = total(half, c)
+
+                over_cols(k, work)
+                if turn == 0:
+                    zh_copy(k).start()
+            return
         if early(k):
             for slot in (DIRECT_DOWN, SECOND_UP, DIRECT_UP, SECOND_DOWN):
                 arrived(k, X_RING + slot, x_in(k, slot))
@@ -357,7 +417,7 @@
         stages[stage](k)
 
     for k in range(len(CHUNKS)):
-        for slot in range(6):
+        for slot in range(3 if direct(k) else 6):
             y_copy(k, slot).wait_send()
             x_copy(k, slot).wait_send()
         zl_copy(k).wait_send()
@@ -389,7 +449,7 @@
 
 def per_device(grad_parts, params, first_moment, second_moment, generator):
     width = params.shape[2]
-    assert sum(tiles for _, _, tiles in CHUNKS) * TILE == width
+    assert sum(tiles for _, _, _, tiles in CHUNKS) * TILE == width
     n = len(CHUNKS)
     any_spec = pl.BlockSpec(memory_space=pl.ANY)
     f32 = jnp.float32

time: 144 us -> 134 us (0.931)
  Pallas kernels: 141 us -> 132 us
    pallas_call x1, Pallas kernels: 138 us -> 129 us  [per_device(): pl.pallas_call(kernel, out_shape=tuple((pltpu.VMEM(out.shape, out.dtype)...]
where the time goes in v3:
time: 134 us; the launch traced here: 133 us
  Pallas kernels  132 us (99%)
    pallas_call x1, Pallas kernels, per_device(): pl.pallas_call(kernel, out_shape=tuple((pltpu.VMEM(out.shape, out.dtype)...  129 us
    pallas_call x1, Pallas kernels, per_device(): pl.pallas_call(copy_out, out_shape=outs, in_specs=[any_spec] * 4, out_spe...  2.97 us

profile of v3, /device:TPU:1, one launch (start us, length us, event | category | flops | bytes accessed | tf_op | source)
XLA Modules:
  0.0 132.7 jit_solution(5378752552159559200)
XLA Ops:
  0.6 129.1 %adam_parity.1 = (f32[1,64,7168]{2,1,0:T(8,128)S(1)}, f32[1,64,7168]{2,1,0:T(8,128)S(1)}, f32[1,64,7168]{2,1,0:T(8,128)S(1)}, f32[1,1,3,16,7168]{4,3,2,1,0:T(8,128)S(1)}) custom-call(f32[4,2,64,7168]{3,2,1,0:T(8,128)} %bitcast.1, f32[1,64,7168]{2,1,0:T(8,128)} %p_ref.1, f32[1,64,7168]{2,1,0:T(8,128)} %m_ref.1, f32[1,64,7168]{2,1,0:T(8,128)} %v_ref.1, ...), custom_call_target="tpu_custom_call" | custom-call | flops 100000000 | bytes 60000000 | tf_op jit(solution)/shard_map/adam_parity/pallas_call | solution.py:457
  129.7 3.0 %copy_out.1 = (f32[1,64,7168]{2,1,0:T(8,128)}, f32[1,64,7168]{2,1,0:T(8,128)}, f32[1,64,7168]{2,1,0:T(8,128)}, f32[1,1,3,16,7168]{4,3,2,1,0:T(8,128)}) custom-call(f32[1,64,7168]{2,1,0:T(8,128)S(1)} %get-tuple-element.8.refs_0_, f32[1,64,7168]{2,1,0:T(8,128)S(1)} %get-tuple-element.9.refs_1_, f32[1,64,7168]{2,1,0:T(8,128)S(1)} %get-tuple-element.10.refs_2_, ...), custom_call_target="tpu_custom_call" | custom-call | bytes 13800000 | tf_op jit(solution)/shard_map/copy_out/pallas_call | solution.py:482

commit v4 on v3

--- a/solution.py
+++ b/solution.py
@@ -11,31 +11,29 @@
 TILE = 128
 
 CHUNKS = (
-    (0, 0, 0, 6), (0, 0, 0, 7), (1, 0, 0, 8), (0, 0, 0, 1), (0, 0, 0, 6), (0, 0, 0, 6), (0, 1, 0, 3),
-    (0, 0, 0, 3), (1, 0, 0, 4), (0, 1, 0, 2), (0, 0, 0, 2), (0, 1, 0, 2), (1, 1, 0, 3), (1, 0, 0, 1),
-    (1, 1, 1, 2),
+    (0, 0, 0, 0, 8), (1, 0, 0, 0, 3), (0, 0, 0, 0, 6), (1, 0, 0, 0, 6), (0, 0, 0, 0, 6), (1, 1, 0, 0, 3), (0, 0, 0, 0, 5),
+    (1, 0, 0, 0, 2), (0, 0, 0, 0, 6), (1, 1, 0, 0, 3), (0, 0, 0, 0, 3), (0, 1, 0, 0, 2), (1, 1, 0, 0, 1), (0, 1, 0, 1, 2),
 )
 BEGIN, ZSUM, YRELAY, YFINAL, ADAM, WEIGH, XRELAY, XFINAL, FINISH = range(9)
 ORDER = (
-    (BEGIN, 2), (BEGIN, 0), (YRELAY, 0), (BEGIN, 1), (YFINAL, 0), (YRELAY, 1),
-    (BEGIN, 8), (ZSUM, 2), (ADAM, 0), (YFINAL, 1), (BEGIN, 3), (WEIGH, 0),
-    (YRELAY, 2), (YRELAY, 3), (BEGIN, 4), (XRELAY, 0), (ADAM, 2), (BEGIN, 12),
-    (YFINAL, 3), (WEIGH, 2), (ADAM, 1), (YRELAY, 4), (XFINAL, 0), (WEIGH, 1),
-    (BEGIN, 5), (XRELAY, 2), (BEGIN, 13), (YFINAL, 4), (ADAM, 3), (WEIGH, 3),
-    (YRELAY, 5), (FINISH, 0), (XRELAY, 1), (BEGIN, 14), (BEGIN, 6), (ADAM, 4),
-    (YFINAL, 5), (BEGIN, 7), (XFINAL, 2), (WEIGH, 4), (YRELAY, 6), (XRELAY, 3),
-    (YRELAY, 7), (XFINAL, 1), (ADAM, 5), (ZSUM, 8), (XRELAY, 4), (YFINAL, 6),
-    (WEIGH, 5), (BEGIN, 9), (FINISH, 2), (YFINAL, 7), (XFINAL, 3), (YRELAY, 8),
-    (FINISH, 1), (XFINAL, 4), (BEGIN, 10), (YRELAY, 9), (ADAM, 6), (XRELAY, 5),
-    (ADAM, 8), (ADAM, 7), (BEGIN, 11), (FINISH, 3), (YRELAY, 10), (WEIGH, 8),
-    (WEIGH, 7), (YFINAL, 9), (FINISH, 4), (ZSUM, 12), (YRELAY, 11), (XFINAL, 5),
-    (WEIGH, 6), (XRELAY, 8), (YFINAL, 10), (ADAM, 9), (ZSUM, 13), (YRELAY, 12),
-    (ZSUM, 14), (YFINAL, 11), (XRELAY, 7), (YRELAY, 13), (FINISH, 5), (ADAM, 10),
-    (ADAM, 12), (XRELAY, 6), (WEIGH, 10), (WEIGH, 9), (ADAM, 13), (ADAM, 11),
-    (ADAM, 14), (XFINAL, 8), (XFINAL, 7), (WEIGH, 13), (XFINAL, 6), (XRELAY, 10),
-    (WEIGH, 12), (XRELAY, 9), (XRELAY, 13), (WEIGH, 11), (XFINAL, 10), (XRELAY, 12),
-    (WEIGH, 14), (XFINAL, 9), (FINISH, 8), (XFINAL, 13), (XRELAY, 11), (FINISH, 7),
-    (XFINAL, 12), (FINISH, 10), (FINISH, 13), (XFINAL, 11), (XFINAL, 14),
+    (BEGIN, 0), (BEGIN, 1), (BEGIN, 3), (ZSUM, 1), (YRELAY, 0), (YRELAY, 1),
+    (BEGIN, 2), (YFINAL, 0), (YRELAY, 2), (BEGIN, 5), (ZSUM, 3), (ADAM, 1),
+    (WEIGH, 1), (BEGIN, 4), (ADAM, 0), (YFINAL, 2), (BEGIN, 7), (XRELAY, 1),
+    (BEGIN, 9), (WEIGH, 0), (YRELAY, 3), (YRELAY, 4), (XRELAY, 0), (ZSUM, 5),
+    (BEGIN, 6), (ADAM, 2), (WEIGH, 2), (ADAM, 3), (WEIGH, 3), (YRELAY, 5),
+    (YFINAL, 4), (BEGIN, 12), (XRELAY, 2), (YRELAY, 6), (XFINAL, 1), (XRELAY, 3),
+    (BEGIN, 8), (ADAM, 4), (ADAM, 5), (YFINAL, 6), (WEIGH, 4), (XFINAL, 0),
+    (YRELAY, 8), (XFINAL, 2), (WEIGH, 5), (ZSUM, 9), (BEGIN, 10), (XRELAY, 4),
+    (ADAM, 6), (ZSUM, 12), (WEIGH, 6), (YFINAL, 8), (XFINAL, 3), (YRELAY, 9),
+    (XRELAY, 5), (YRELAY, 10), (XFINAL, 4), (XRELAY, 6), (BEGIN, 11), (ADAM, 8),
+    (BEGIN, 13), (WEIGH, 8), (YFINAL, 10), (YRELAY, 11), (ADAM, 9), (ZSUM, 7),
+    (ADAM, 10), (YRELAY, 13), (XRELAY, 8), (XFINAL, 6), (FINISH, 4), (YRELAY, 12),
+    (YFINAL, 11), (YRELAY, 7), (WEIGH, 10), (YFINAL, 13), (ADAM, 12), (WEIGH, 9),
+    (ADAM, 7), (ADAM, 11), (WEIGH, 7), (ADAM, 13), (FINISH, 6), (FINISH, 1),
+    (XFINAL, 8), (XRELAY, 10), (WEIGH, 12), (XRELAY, 7), (XRELAY, 9), (WEIGH, 11),
+    (XFINAL, 10), (WEIGH, 13), (XFINAL, 5), (FINISH, 3), (FINISH, 0), (XRELAY, 12),
+    (XFINAL, 7), (XFINAL, 9), (XRELAY, 11), (XFINAL, 12), (FINISH, 8), (FINISH, 2),
+    (FINISH, 10), (FINISH, 7), (XFINAL, 13), (XFINAL, 11),
 )
 
 RELAY_UP, RELAY_DOWN, DIRECT_UP, DIRECT_DOWN, SECOND_UP, SECOND_DOWN = range(6)
@@ -77,15 +75,15 @@
     pl.semaphore_wait(barrier, len(peers))
 
     starts = []
-    for _, _, _, tiles in CHUNKS:
+    for _, _, _, _, tiles in CHUNKS:
         starts.append(starts[-1] + last if starts else 0)
         last = tiles * TILE
 
     def cols(k):
-        return pl.ds(starts[k], CHUNKS[k][3] * TILE)
+        return pl.ds(starts[k], CHUNKS[k][4] * TILE)
 
     def over_cols(k, work):
-        start, tiles = starts[k], CHUNKS[k][3]
+        start, tiles = starts[k], CHUNKS[k][4]
         step = 2 * TILE if tiles % 2 == 0 else TILE
         n = tiles * TILE // step
         if n == 1:
@@ -109,23 +107,26 @@
     def early(k):
         return CHUNKS[k][1]
 
-    def direct(k):
+    def y_direct(k):
         return CHUNKS[k][2]
 
-    def ring_slots(k):
-        return (TO_UP, TO_DOWN, TO_FAR) if direct(k) else (RELAY_UP, RELAY_DOWN, DIRECT_UP, DIRECT_DOWN)
+    def x_direct(k):
+        return CHUNKS[k][3]
+
+    def first_slots(direct):
+        return (TO_UP, TO_DOWN, TO_FAR) if direct else (RELAY_UP, RELAY_DOWN, DIRECT_UP, DIRECT_DOWN)
 
     def y_place(k, slot):
         return (4 + slot // 2, (slot % 2) * 32, 32) if z_first(k) else (slot, 0, 64)
 
     def y_in(k, slot):
-        if direct(k):
+        if y_direct(k):
             return got.at[4 + slot, :, cols(k)] if z_first(k) else got.at[2 * slot:2 * slot + 2, :, cols(k)]
         i, r, n = y_place(k, slot)
         return got.at[i, pl.ds(r, n), cols(k)]
 
     def y_copy(k, slot):
-        if direct(k):
+        if y_direct(k):
             block = (y_up, y_down, y_far)[slot]
             src = got.at[block, :, cols(k)] if z_first(k) else g_ref.at[block, :, :, cols(k)]
             return remote(k, slot, src, y_in(k, slot), (to_y_up, to_y_down, to_y_far)[slot])
@@ -165,12 +166,12 @@
         return wgt.at[block, half, :, :, cols(k)]
 
     def x_in(k, slot):
-        if direct(k):
+        if x_direct(k):
             return xr.at[2 * slot, :, :, cols(k)] if early(k) else xr.at[2 * slot:2 * slot + 2, :, :, cols(k)]
         return xr.at[slot, :, pl.ds(0, 8 if early(k) else 16), cols(k)]
 
     def x_copy(k, slot):
-        if direct(k):
+        if x_direct(k):
             block = (x_up, x_down, x_far)[slot]
             src = wgt.at[block, 0, :, :, cols(k)] if early(k) else wgt.at[block, :, :, :, cols(k)]
             return remote(k, X_RING + slot, src, x_in(k, slot), (to_x_up, to_x_down, to_x_far)[slot])
@@ -195,7 +196,7 @@
         c = cols(k)
         if z_first(k):
             pairs = [(g_ref.at[:, zl, :, c], own.at[:, :, c])]
-        elif direct(k):
+        elif y_direct(k):
             pairs = [(g_ref.at[y, :, :, c], own.at[0:2, :, c])]
         else:
             pairs = [
@@ -211,7 +212,7 @@
         if z_first(k):
             zl_copy(k).start()
         else:
-            for slot in ring_slots(k):
+            for slot in first_slots(y_direct(k)):
                 y_copy(k, slot).start()
         for copy in loads(k):
             copy().start()
@@ -226,7 +227,7 @@
 
             over_cols(k, work)
 
-        if direct(k):
+        if y_direct(k):
             for slot, block in ((TO_FAR, y_far), (TO_UP, y_up), (TO_DOWN, y_down)):
                 add(block)
                 y_copy(k, slot).start()
@@ -258,17 +259,17 @@
             y_copy(k, onward).start()
 
     def yfinal(k):
-        loads(k)[0 if direct(k) else 2]().wait()
-        if direct(k):
+        loads(k)[0 if y_direct(k) else 2]().wait()
+        if y_direct(k):
             for slot in range(3):
                 arrived(k, slot, y_in(k, slot))
         for turn, half in enumerate((1 - zl, zl)):
-            if not direct(k):
+            if not y_direct(k):
                 for slot in (3 - half, 4 + half):
                     arrived(k, slot, got.at[slot, :, cols(k)])
 
             def work(c):
-                if direct(k):
+                if y_direct(k):
                     own[half, :, c] = own[half, :, c] + got[half, :, c] + got[2 + half, :, c] + got[4 + half, :, c]
                 else:
                     own[half, :, c] = own[half, :, c] + got[3 - half, :, c] + got[4 + half, :, c]
@@ -281,7 +282,7 @@
         for copy in loads(k)[-3:]:
             copy().wait()
         if z_first(k):
-            for slot in range(3) if direct(k) else (DIRECT_DOWN, SECOND_UP, DIRECT_UP, SECOND_DOWN):
+            for slot in range(3) if y_direct(k) else (DIRECT_DOWN, SECOND_UP, DIRECT_UP, SECOND_DOWN):
                 arrived(k, slot, y_in(k, slot))
         else:
             arrived(k, Z_LO, got.at[6, :, cols(k)])
@@ -291,7 +292,7 @@
         def work(c):
             for q in range(4):
                 r = pl.ds(q * 16, 16)
-                if z_first(k) and direct(k):
+                if z_first(k) and y_direct(k):
                     grad = got[y, r, c] + got[4, r, c] + got[5, r, c] + got[6, r, c]
                 elif z_first(k):
                     grad = got[y, r, c]
@@ -339,7 +340,7 @@
                         wgt[j, half, :, :, c] = gen_ref[j, rec] * mine + gen_ref[j, rec_core] * other
 
         over_cols(k, work)
-        for slot in ring_slots(k):
+        for slot in first_slots(x_direct(k)):
             x_copy(k, slot).start()
 
     def xrelay(k):
@@ -357,7 +358,7 @@
             x_copy(k, onward).start()
 
     def xfinal(k):
-        if direct(k):
+        if x_direct(k):
             for slot in range(3):
                 arrived(k, X_RING + slot, x_in(k, slot))
 
@@ -417,8 +418,9 @@
         stages[stage](k)
 
     for k in range(len(CHUNKS)):
-        for slot in range(3 if direct(k) else 6):
+        for slot in range(3 if y_direct(k) else 6):
             y_copy(k, slot).wait_send()
+        for slot in range(3 if x_direct(k) else 6):
             x_copy(k, slot).wait_send()
         zl_copy(k).wait_send()
         for copy in group_copies(k):
@@ -449,7 +451,7 @@
 
 def per_device(grad_parts, params, first_moment, second_moment, generator):
     width = params.shape[2]
-    assert sum(tiles for _, _, _, tiles in CHUNKS) * TILE == width
+    assert sum(tiles for _, _, _, _, tiles in CHUNKS) * TILE == width
     n = len(CHUNKS)
     any_spec = pl.BlockSpec(memory_space=pl.ANY)
     f32 = jnp.float32

time: 134 us -> 132 us (0.985); the launches traced: 133 us -> 132 us
  no operation moved by 1% of the time
where the time goes in v4:
time: 132 us
  Pallas kernels  132 us (100%)
    pallas_call x1, Pallas kernels, per_device(): pl.pallas_call(kernel, out_shape=tuple((pltpu.VMEM(out.shape, out.dtype)...  129 us
    pallas_call x1, Pallas kernels, per_device(): pl.pallas_call(copy_out, out_shape=outs, in_specs=[any_spec] * 4, out_spe...  2.97 us

profile of v4, /device:TPU:1, one launch (start us, length us, event | category | flops | bytes accessed | tf_op | source)
XLA Modules:
  0.0 132.3 jit_solution(668996183464497696)
XLA Ops:
  0.6 128.6 %adam_parity.1 = (f32[1,64,7168]{2,1,0:T(8,128)S(1)}, f32[1,64,7168]{2,1,0:T(8,128)S(1)}, f32[1,64,7168]{2,1,0:T(8,128)S(1)}, f32[1,1,3,16,7168]{4,3,2,1,0:T(8,128)S(1)}) custom-call(f32[4,2,64,7168]{3,2,1,0:T(8,128)} %bitcast.1, f32[1,64,7168]{2,1,0:T(8,128)} %p_ref.1, f32[1,64,7168]{2,1,0:T(8,128)} %m_ref.1, f32[1,64,7168]{2,1,0:T(8,128)} %v_ref.1, ...), custom_call_target="tpu_custom_call" | custom-call | flops 100000000 | bytes 60000000 | tf_op jit(solution)/shard_map/adam_parity/pallas_call | solution.py:459
  129.3 3.0 %copy_out.1 = (f32[1,64,7168]{2,1,0:T(8,128)}, f32[1,64,7168]{2,1,0:T(8,128)}, f32[1,64,7168]{2,1,0:T(8,128)}, f32[1,1,3,16,7168]{4,3,2,1,0:T(8,128)}) custom-call(f32[1,64,7168]{2,1,0:T(8,128)S(1)} %get-tuple-element.8.refs_0_, f32[1,64,7168]{2,1,0:T(8,128)S(1)} %get-tuple-element.9.refs_1_, f32[1,64,7168]{2,1,0:T(8,128)S(1)} %get-tuple-element.10.refs_2_, ...), custom_call_target="tpu_custom_call" | custom-call | bytes 13800000 | tf_op jit(solution)/shard_map/copy_out/pallas_call | solution.py:484

commit v5 on v4

--- a/solution.py
+++ b/solution.py
@@ -41,6 +41,7 @@
 Z_LO, CORE, X_RING, Z_HI, Z_HI_CORE = 6, 7, 8, 14, 15
 SLOTS = 16
 LOADS = 6
+SETTLE = 16
 
 
 def kernel(
@@ -68,8 +69,23 @@
 
     to_x_far = (dp, x_far * 4 + zh * 2 + core)
 
+    def z_first(k):
+        return CHUNKS[k][0]
+
+    def early(k):
+        return CHUNKS[k][1]
+
+    def y_direct(k):
+        return CHUNKS[k][2]
+
+    def x_direct(k):
+        return CHUNKS[k][3]
+
     barrier = pltpu.get_barrier_semaphore()
-    peers = (to_y_up, to_y_down, to_y_far, to_zl, to_core, to_zh, to_both, to_x_up, to_x_down, to_x_far)
+    peers = [to_y_up, to_y_down, to_zl, to_core, to_zh, to_x_up, to_x_down]
+    peers += [to_both] if any(early(k) for k in range(len(CHUNKS))) else []
+    peers += [to_y_far] if any(y_direct(k) for k in range(len(CHUNKS))) else []
+    peers += [to_x_far] if any(x_direct(k) for k in range(len(CHUNKS))) else []
     for peer in peers:
         pl.semaphore_signal(barrier, inc=1, device_id=peer, device_id_type=MESH)
     pl.semaphore_wait(barrier, len(peers))
@@ -100,18 +116,6 @@
             src_ref=src, dst_ref=dst, send_sem=ssem.at[k, slot], recv_sem=rsem.at[k, slot],
             device_id=device, device_id_type=MESH,
         )
-
-    def z_first(k):
-        return CHUNKS[k][0]
-
-    def early(k):
-        return CHUNKS[k][1]
-
-    def y_direct(k):
-        return CHUNKS[k][2]
-
-    def x_direct(k):
-        return CHUNKS[k][3]
 
     def first_slots(direct):
         return (TO_UP, TO_DOWN, TO_FAR) if direct else (RELAY_UP, RELAY_DOWN, DIRECT_UP, DIRECT_DOWN)
@@ -410,23 +414,34 @@
 
         over_cols(k, work)
 
+    def gradient_sent(k):
+        for slot in range(3 if y_direct(k) else 6):
+            y_copy(k, slot).wait_send()
+        zl_copy(k).wait_send()
+
+    def parity_sent(k):
+        for copy in group_copies(k):
+            copy.wait_send()
+        for slot in range(3 if x_direct(k) else 6):
+            x_copy(k, slot).wait_send()
+        if not early(k):
+            zh_copy(k).wait_send()
+
     stages = {
         BEGIN: begin, ZSUM: zsum, YRELAY: yrelay, YFINAL: yfinal, ADAM: adam,
         WEIGH: weigh, XRELAY: xrelay, XFINAL: xfinal, FINISH: finish,
     }
-    for stage, k in ORDER:
+    last = {k: at for at, (_, k) in enumerate(ORDER)}
+    for at, (stage, k) in enumerate(ORDER):
         stages[stage](k)
-
-    for k in range(len(CHUNKS)):
-        for slot in range(3 if y_direct(k) else 6):
-            y_copy(k, slot).wait_send()
-        for slot in range(3 if x_direct(k) else 6):
-            x_copy(k, slot).wait_send()
-        zl_copy(k).wait_send()
-        for copy in group_copies(k):
-            copy.wait_send()
-        if not early(k):
-            zh_copy(k).wait_send()
+        if stage == WEIGH:
+            gradient_sent(k)
+        for j in range(len(CHUNKS)):
+            if last[j] + SETTLE == at:
+                parity_sent(j)
+    for j in range(len(CHUNKS)):
+        if last[j] + SETTLE >= len(ORDER):
+            parity_sent(j)
 
 
 def copy_out(*refs):

time: 132 us -> 132 us (level)
  no operation moved by 1% of the time
where the time goes in v5:
time: 132 us
  Pallas kernels  131 us (99%)
    pallas_call x1, Pallas kernels, per_device(): pl.pallas_call(kernel, out_shape=tuple((pltpu.VMEM(out.shape, out.dtype)...  128 us
    pallas_call x1, Pallas kernels, per_device(): pl.pallas_call(copy_out, out_shape=outs, in_specs=[any_spec] * 4, out_spe...  2.97 us

profile of v5, /device:TPU:1, one launch (start us, length us, event | category | flops | bytes accessed | tf_op | source)
XLA Modules:
  0.0 132.0 jit_solution(10447485937638619208)
XLA Ops:
  0.6 128.4 %adam_parity.1 = (f32[1,64,7168]{2,1,0:T(8,128)S(1)}, f32[1,64,7168]{2,1,0:T(8,128)S(1)}, f32[1,64,7168]{2,1,0:T(8,128)S(1)}, f32[1,1,3,16,7168]{4,3,2,1,0:T(8,128)S(1)}) custom-call(f32[4,2,64,7168]{3,2,1,0:T(8,128)} %bitcast.1, f32[1,64,7168]{2,1,0:T(8,128)} %p_ref.1, f32[1,64,7168]{2,1,0:T(8,128)} %m_ref.1, f32[1,64,7168]{2,1,0:T(8,128)} %v_ref.1, ...), custom_call_target="tpu_custom_call" | custom-call | flops 100000000 | bytes 60000000 | tf_op jit(solution)/shard_map/adam_parity/pallas_call | solution.py:474
  129.1 3.0 %copy_out.1 = (f32[1,64,7168]{2,1,0:T(8,128)}, f32[1,64,7168]{2,1,0:T(8,128)}, f32[1,64,7168]{2,1,0:T(8,128)}, f32[1,1,3,16,7168]{4,3,2,1,0:T(8,128)}) custom-call(f32[1,64,7168]{2,1,0:T(8,128)S(1)} %get-tuple-element.8.refs_0_, f32[1,64,7168]{2,1,0:T(8,128)S(1)} %get-tuple-element.9.refs_1_, f32[1,64,7168]{2,1,0:T(8,128)S(1)} %get-tuple-element.10.refs_2_, ...), custom_call_target="tpu_custom_call" | custom-call | bytes 13800000 | tf_op jit(solution)/shard_map/copy_out/pallas_call | solution.py:499

commit v6 on v5

--- a/solution.py
+++ b/solution.py
@@ -81,15 +81,6 @@
     def x_direct(k):
         return CHUNKS[k][3]
 
-    barrier = pltpu.get_barrier_semaphore()
-    peers = [to_y_up, to_y_down, to_zl, to_core, to_zh, to_x_up, to_x_down]
-    peers += [to_both] if any(early(k) for k in range(len(CHUNKS))) else []
-    peers += [to_y_far] if any(y_direct(k) for k in range(len(CHUNKS))) else []
-    peers += [to_x_far] if any(x_direct(k) for k in range(len(CHUNKS))) else []
-    for peer in peers:
-        pl.semaphore_signal(barrier, inc=1, device_id=peer, device_id_type=MESH)
-    pl.semaphore_wait(barrier, len(peers))
-
     starts = []
     for _, _, _, _, tiles in CHUNKS:
         starts.append(starts[-1] + last if starts else 0)
@@ -212,14 +203,17 @@
         pairs += [(src.at[0, :, c], dst.at[0, :, c]) for src, dst in state]
         return [functools.partial(pltpu.make_async_copy, src, dst, lsem.at[k, i]) for i, (src, dst) in enumerate(pairs)]
 
+    loaded = []
+
     def begin(k):
         if z_first(k):
             zl_copy(k).start()
         else:
             for slot in first_slots(y_direct(k)):
                 y_copy(k, slot).start()
-        for copy in loads(k):
-            copy().start()
+        if k not in loaded:
+            for copy in loads(k):
+                copy().start()
 
     def zsum(k):
         loads(k)[0]().wait()
@@ -431,6 +425,21 @@
         BEGIN: begin, ZSUM: zsum, YRELAY: yrelay, YFINAL: yfinal, ADAM: adam,
         WEIGH: weigh, XRELAY: xrelay, XFINAL: xfinal, FINISH: finish,
     }
+    barrier = pltpu.get_barrier_semaphore()
+    peers = [to_y_up, to_y_down, to_zl, to_core, to_zh, to_x_up, to_x_down]
+    peers += [to_both] if any(early(k) for k in range(len(CHUNKS))) else []
+    peers += [to_y_far] if any(y_direct(k) for k in range(len(CHUNKS))) else []
+    peers += [to_x_far] if any(x_direct(k) for k in range(len(CHUNKS))) else []
+    for peer in peers:
+        pl.semaphore_signal(barrier, inc=1, device_id=peer, device_id_type=MESH)
+    for stage, k in ORDER:
+        if stage != BEGIN:
+            break
+        loaded.append(k)
+        for copy in loads(k):
+            copy().start()
+    pl.semaphore_wait(barrier, len(peers))
+
     last = {k: at for at, (_, k) in enumerate(ORDER)}
     for at, (stage, k) in enumerate(ORDER):
         stages[stage](k)

time: 132 us -> 132 us (level)
  no operation moved by 1% of the time
where the time goes in v6:
time: 132 us
  Pallas kernels  131 us (99%)
    pallas_call x1, Pallas kernels, per_device(): pl.pallas_call(kernel, out_shape=tuple((pltpu.VMEM(out.shape, out.dtype)...  128 us
    pallas_call x1, Pallas kernels, per_device(): pl.pallas_call(copy_out, out_shape=outs, in_specs=[any_spec] * 4, out_spe...  2.97 us

profile of v6, /device:TPU:1, one launch (start us, length us, event | category | flops | bytes accessed | tf_op | source)
XLA Modules:
  0.0 132.1 jit_solution(10233124946603122001)
XLA Ops:
  0.6 128.4 %adam_parity.1 = (f32[1,64,7168]{2,1,0:T(8,128)S(1)}, f32[1,64,7168]{2,1,0:T(8,128)S(1)}, f32[1,64,7168]{2,1,0:T(8,128)S(1)}, f32[1,1,3,16,7168]{4,3,2,1,0:T(8,128)S(1)}) custom-call(f32[4,2,64,7168]{3,2,1,0:T(8,128)} %bitcast.1, f32[1,64,7168]{2,1,0:T(8,128)} %p_ref.1, f32[1,64,7168]{2,1,0:T(8,128)} %m_ref.1, f32[1,64,7168]{2,1,0:T(8,128)} %v_ref.1, ...), custom_call_target="tpu_custom_call" | custom-call | flops 100000000 | bytes 60000000 | tf_op jit(solution)/shard_map/adam_parity/pallas_call | solution.py:483
  129.1 3.0 %copy_out.1 = (f32[1,64,7168]{2,1,0:T(8,128)}, f32[1,64,7168]{2,1,0:T(8,128)}, f32[1,64,7168]{2,1,0:T(8,128)}, f32[1,1,3,16,7168]{4,3,2,1,0:T(8,128)}) custom-call(f32[1,64,7168]{2,1,0:T(8,128)S(1)} %get-tuple-element.8.refs_0_, f32[1,64,7168]{2,1,0:T(8,128)S(1)} %get-tuple-element.9.refs_1_, f32[1,64,7168]{2,1,0:T(8,128)S(1)} %get-tuple-element.10.refs_2_, ...), custom_call_target="tpu_custom_call" | custom-call | bytes 13800000 | tf_op jit(solution)/shard_map/copy_out/pallas_call | solution.py:508
